TPU v7x, 256 devices: a whole 4x4x8 slice. The times are simulated.
256 devices in a mesh: ctx: 32 (over x, z_lo, core), exp: 8 (over y, z_hi).
Axes of the slice: x: 4, y: 4, z: 8 (z_hi: 2, z_lo: 4; z = z_hi * 4 + z_lo), core: 2. Of those that a mesh axis runs over, the one named last changes fastest.
Arguments:
- queries: bfloat16 [2048, 6144], P('ctx', 'exp'), may hold values from -120 to 120
- rotated_key_cache: bfloat16 [8192, 1024], P('ctx', 'exp'), may hold values from -4.1 to 4.1
- value_cache_rows: bfloat16 [8192, 1024], P('ctx', 'exp'), may hold values from -6 to 6
- kv_pos: int32 [8192], P('ctx'), may hold values from 0 to 8191, as said below
- q_pos: int32 [2048], P('ctx'), may hold values from 4096 to 8191
- residual: bfloat16 [2048, 6144], P('exp', 'ctx'), may hold values from -30 to 30
- w_out: bfloat16 [6144, 6144], P('exp', 'ctx'), may hold values from -0.078125 to 0.078125
- norm_gain: bfloat16 [6144], P('ctx'), may hold values from 0.099609375 to 1.8984375
- routes: int32 [2048, 2], P('exp'), may hold values from 0 to 7, all different within a row; in each aligned block of 256 rows (0 to 255, 256 to 511, ...) at most 192 rows name the same one
- gate_probs: float32 [2048, 2], P('exp'), may hold values from 0.1 to 1
- w_gate: bfloat16 [8, 6144, 8192], P('exp', None, 'ctx'), may hold values from -0.078125 to 0.078125
- w_up: bfloat16 [8, 6144, 8192], P('exp', None, 'ctx'), may hold values from -0.078125 to 0.078125
- w_down: bfloat16 [8, 8192, 6144], P('exp', 'ctx'), may hold values from -0.0625 to 0.0625
Outputs:
- attended: bfloat16 [2048, 6144], P('ctx', 'exp')
- mixed: bfloat16 [2048, 6144], P('exp', 'ctx')
Inputs may be any that keep to these rules, and one draw needn't show every extreme that they name: `routes`: in each aligned block of 256 rows (the tokens of one index of exp) no expert is named by more than 192 rows; the two experts of a row differ. `kv_pos`: each position 0 to 8191 appears once; each aligned run of 128 slots holds consecutive positions in increasing order.
All inputs are finite; a program needn't handle non-finite values.
Results may differ from a plain program's by a relative error of at most 0.015.
Values may be sent and summed in bfloat16 or wider, within the bound.
A program may use at most 128 MiB of HBM per device.

v0:
```python
import jax
import jax.numpy as jnp
from jax import lax
from jax.experimental import pallas as pl
from jax.experimental.pallas import tpu as pltpu
from jax.sharding import Mesh
from jax.sharding import PartitionSpec as P

MESH = pl.DeviceIdType.MESH
DMA = pltpu.SemaphoreType.DMA
D = 6144
NX, NZ, NY = 4, 4, 4
STEPS = 8
EXPERTS = 8
neg_big = -1e30
epsilon = 1e-05
LOG2E = 1.4426950408889634

TOK, HEAD, HEADS, POS, BLOCK, SLOTS, WIDE, HID = 64, 128, 6, 256, 256, 96, 384, 512
JOINED = HEADS * HEAD
FEATS = WIDE // 2
DEEP = POS + 16

bf16, f32 = jnp.bfloat16, jnp.float32


def vmem(*shape, kind=bf16):
    return pltpu.VMEM(shape, kind)


SCRATCH = {
    "held": vmem(2 * NX * NZ, DEEP, 2 * HEAD),
    "q_rows": vmem(TOK * HEADS, HEAD),
    "limit": vmem(2 * TOK, 1, kind=f32),
    "top": vmem(TOK * HEADS, HEAD, kind=f32),
    "acc": vmem(TOK * HEADS, 2 * HEAD, kind=f32),
    "gain_squares": vmem(NX * NZ, 1, WIDE, kind=f32),
    "slab": vmem(NX * NZ * TOK, JOINED),
    "wo": vmem(WIDE, JOINED),
    "res": vmem(WIDE, BLOCK),
    "res_rows": vmem(BLOCK, WIDE),
    "leaving": vmem(NX, NZ * TOK, WIDE),
    "pieces": vmem(EXPERTS, 2 * TOK, WIDE),
    "stream": vmem(2 * TOK, WIDE, kind=f32),
    "both": vmem(BLOCK, WIDE),
    "placer": vmem(EXPERTS * SLOTS, BLOCK),
    "picker": vmem(2, BLOCK, EXPERTS * SLOTS),
    "rows_out": vmem(EXPERTS, SLOTS, WIDE),
    "rows_in": vmem(STEPS, SLOTS, WIDE),
    "spread": vmem(STEPS, NX * NZ, SLOTS, WIDE),
    "part": vmem(STEPS, NX * NZ, SLOTS, WIDE),
    "relay": vmem(STEPS, 2, NZ, SLOTS // 2, WIDE),
    "from_x": vmem(STEPS, 2, NZ, SLOTS, WIDE),
    "mine": vmem(STEPS, NZ - 1, SLOTS, WIDE),
    "from_z": vmem(STEPS, NZ - 1, SLOTS, WIDE),
    "done": vmem(STEPS, SLOTS, WIDE),
    "wg": vmem(D, HID),
    "wu": vmem(D, HID),
    "wd": vmem(HID, D),
    "gate_sum": vmem(SLOTS, HID, kind=f32),
    "up_sum": vmem(SLOTS, HID, kind=f32),
    "squares": vmem(SLOTS, 128, kind=f32),
    "act": vmem(SLOTS, HID),
    "returned": vmem(EXPERTS, SLOTS, WIDE),
    "give": vmem(BLOCK, FEATS, kind=f32),
    "got": vmem(BLOCK, FEATS, kind=f32),
    "w_sem": DMA((4,)),
    "own_sem": DMA((STEPS,)),
}
KINDS = {
    "kz": 3, "kx": 4, "kf": 4, "kk": 8, "kh": 4,
    "az": 3, "ax": 4, "af": 1, "ap": 1, "ab": 1,
    "dd": 8, "rt": 1, "ge": 1, "two": 1, "tre": 1, "twg": 1, "twu": 1, "twd": 1,
    "ez": 3 * STEPS, "ex": 4 * STEPS, "ef": STEPS,
    "er": 4 * STEPS, "eu": STEPS, "ev": 4 * STEPS, "eq": STEPS,
}
SCRATCH["sent"] = DMA((len(KINDS),))
for kind, many in KINDS.items():
    SCRATCH[kind] = DMA((many,))


def remote(src, dst, send_sem, recv_sem, device):
    return pltpu.make_async_remote_copy(
        src_ref=src,
        dst_ref=dst,
        send_sem=send_sem,
        recv_sem=recv_sem,
        device_id=device,
        device_id_type=MESH,
    )


def layer_kernel(
    q_ref, q_pos_ref, k_ref, v_ref, page_ref, gain_ref, res_ref, wo_ref, routes_ref, probs_ref,
    wg_ref, wu_ref, wd_ref, att_ref, mixed_ref, *refs,
):
    at_name = dict(zip(SCRATCH, refs))

    class R:
        pass

    for name, ref in at_name.items():
        setattr(R, name, ref)
    x, z, k, y, w = (lax.axis_index(name) for name in ("x", "z", "k", "y", "w"))
    up, down, across = lax.rem(x + 1, NX), lax.rem(x + 3, NX), lax.rem(x + 2, NX)
    ways = (up, down)
    order = [lax.rem(z + step, NZ) for step in (1, 2, 3, 0)]
    others = [(dy, dw) for dy in range(NY) for dw in range(2) if (dy, dw) != (0, 0)]
    own_expert = 2 * y + w

    kinds = list(KINDS)

    def start(kind, at, src, dst, device):
        remote(src, dst, R.sent.at[kinds.index(kind)], at_name[kind].at[at], device).start()

    def arrived(kind, at, ref):
        remote(ref, ref, R.sent.at[kinds.index(kind)], at_name[kind].at[at], {"x": up}).wait_recv()

    def left(kind, ref):
        remote(ref, ref, R.sent.at[kinds.index(kind)], at_name[kind].at[0], {"x": up}).wait_send()

    def behind(step):
        return lax.rem(z + NZ - step, NZ)

    held = R.held
    own = 2 * (x * NZ + z) + k
    held[own, :POS, :HEAD] = k_ref[...]
    held[own, :POS, HEAD:] = v_ref[...]
    pages = page_ref[...].astype(f32) * (1.0 / 128.0)
    row = lax.broadcasted_iota(jnp.int32, (16, 2 * HEAD), 0)
    lane = lax.broadcasted_iota(jnp.int32, (16, 2 * HEAD), 1)
    numbers = jnp.where(lane == 0, pages[0:1, 0:1], jnp.where(lane == 1, pages[1:2, 0:1], 0.0))
    gain = jnp.concatenate([gain_ref[...].astype(f32), jnp.zeros((1, 2 * HEAD - FEATS), f32)], axis=1)
    extra = jnp.where(row == 0, numbers, jnp.where(row == 1, gain, 0.0))
    held[own, POS:, :] = extra.astype(bf16)

    barrier = pltpu.get_barrier_semaphore()
    peers = [{"x": up}, {"x": down}, {"k": 1 - k}]
    peers += [{"z": lax.rem(z + step, NZ)} for step in range(1, NZ)]
    peers += [{"y": lax.rem(y + dy, NY), "w": lax.rem(w + dw, 2)} for dy, dw in others]
    for device in peers:
        pl.semaphore_signal(barrier, inc=1, device_id=device, device_id_type=MESH)
    pl.semaphore_wait(barrier, len(peers))

    halves = ((0, 144), (144, DEEP - 144))

    def spot(bx, bz, core, half=None):
        where = 2 * (bx * NZ + bz) + core
        if half is None:
            return held.at[where]
        return held.at[where, pl.ds(*halves[half])]

    block = spot(x, z, k)
    for step in range(1, NZ):
        start("kz", step - 1, block, block, {"z": lax.rem(z + step, NZ)})
    for way, goes in enumerate(ways):
        start("kx", 0, block, block, {"x": goes})
    start("kk", 0, block, block, {"k": 1 - k})

    def feats_of(core):
        return pl.ds(pl.multiple_of(core * FEATS, 16), FEATS)

    local_wo = pltpu.make_async_copy(wo_ref, R.wo.at[feats_of(k)], R.w_sem.at[0])
    local_wo.start()
    start("two", 0, wo_ref, R.wo.at[feats_of(k)], {"k": 1 - k})
    R.res[feats_of(k), :] = res_ref[...]
    start("tre", 0, res_ref, R.res.at[feats_of(k)], {"k": 1 - k})

    def upright(rows):
        return jnp.concatenate([rows.astype(f32), jnp.zeros((6, BLOCK), f32)], axis=0).T

    routes = upright(routes_ref[...]).astype(jnp.int32)
    probs = upright(probs_ref[...])
    expert_lane = lax.broadcasted_iota(jnp.int32, (BLOCK, 128), 1)
    named = [(routes[:, c : c + 1] == expert_lane).astype(f32) for c in range(2)]
    before = lax.broadcasted_iota(jnp.int32, (BLOCK, BLOCK), 0) > lax.broadcasted_iota(
        jnp.int32, (BLOCK, BLOCK), 1
    )
    earlier = jnp.dot(
        before.astype(f32).astype(bf16), (named[0] + named[1]).astype(bf16), preferred_element_type=f32
    )
    slot_lane = lax.broadcasted_iota(jnp.int32, (BLOCK, EXPERTS * SLOTS), 1)
    hits = []
    for c in range(2):
        slot = jnp.sum(earlier * named[c], axis=1, keepdims=True).astype(jnp.int32) - k * SLOTS
        ok = (slot >= 0) & (slot < SLOTS)
        hits.append(jnp.where(ok, routes[:, c : c + 1] * SLOTS + slot, -1) == slot_lane)
    placer = jnp.where(hits[0], 1.0, jnp.where(hits[1], 1.0, 0.0))
    R.placer[...] = placer.T.astype(bf16)
    picker = jnp.where(hits[0], probs[:, 0:1], jnp.where(hits[1], probs[:, 1:2], 0.0))
    high = picker.astype(bf16)
    R.picker[0] = high
    R.picker[1] = (picker - high.astype(f32)).astype(bf16)

    for h in range(HEADS):
        R.q_rows[pl.ds(h * TOK, TOK), :] = q_ref[:, pl.ds(h * HEAD, HEAD)]
    R.top[...] = jnp.full_like(R.top, neg_big)
    R.acc[...] = jnp.zeros_like(R.acc)
    limit = jnp.broadcast_to(q_pos_ref[...].astype(f32), (8, TOK)).T[:, 0:1]
    R.limit[...] = jnp.concatenate([limit, limit], axis=0)
    scaling = HEAD**-0.5 * LOG2E
    tile = 2 * TOK

    def attend(bx, bz):
        where = 2 * (bx * NZ + bz)
        terms = []
        steps = lax.broadcasted_iota(jnp.int32, (1, HEAD), 1).astype(f32)
        for core in range(2):
            starts = held[where + core, POS:, :HEAD].astype(f32)
            positions = jnp.concatenate(
                [starts[0:1, 0:1] * 128.0 + steps, starts[0:1, 1:2] * 128.0 + steps], axis=1
            )
            terms.append((held[where + core, :POS, :HEAD], held[where + core, :POS, HEAD:], positions))
        ones = jnp.ones((POS, HEAD), bf16)
        limit = R.limit[...]
        for r in range(TOK * HEADS // tile):
            at = pl.ds(r * tile, tile)
            scores = []
            for keys, _, positions in terms:
                score = lax.dot_general(
                    R.q_rows[at, :], keys, (((1,), (1,)), ((), ())), preferred_element_type=f32
                )
                scores.append(jnp.where(positions <= limit, score * scaling, neg_big))
            most = jnp.maximum(scores[0], scores[1])
            most = jnp.max(jnp.maximum(most[:, :HEAD], most[:, HEAD:]), axis=1, keepdims=True)
            old = R.top[at, :]
            new = jnp.maximum(old, most)
            R.top[at, :] = new
            fade = jnp.exp2(old - new)
            total = R.acc[at, :] * jnp.concatenate([fade, fade], axis=1)
            new = jnp.concatenate([new, new], axis=1)
            for score, (_, values, _) in zip(scores, terms):
                weights = jnp.exp2(score - new).astype(bf16)
                total = total + jnp.dot(
                    weights, jnp.concatenate([values, ones], axis=1), preferred_element_type=f32
                )
            R.acc[at, :] = total

    arrived("kk", 0, spot(x, z, 1 - k))
    attend(x, z)

    @pl.loop(1, NZ)
    def _(step):
        ref = spot(x, behind(step), k)
        arrived("kz", step - 1, ref)
        for way, goes in enumerate(ways):
            start("kx", step, ref, ref, {"x": goes})
        start("kk", step, ref, ref, {"k": 1 - k})

    @pl.loop(0, NZ)
    def _(step):
        bz = behind(step)
        arrived("kx", step, held.at[pl.ds(0, 2)])
        for way, (came, goes) in enumerate(((down, up), (up, down))):
            ref = spot(came, bz, k)
            half = spot(came, bz, k, way)
            start("kf", step, half, half, {"x": goes})
            start("kk", NZ + step, ref, ref, {"k": 1 - k})

        @pl.when(step > 0)
        def _():
            arrived("kk", step, spot(x, bz, 1 - k))
            attend(x, bz)

    @pl.loop(0, NZ)
    def _(step):
        bz = behind(step)
        ref = spot(across, bz, k)
        arrived("kf", step, ref)
        start("kh", step, ref, ref, {"k": 1 - k})
        arrived("kk", NZ + step, held.at[pl.ds(0, 2)])
        for came in (down, up):
            attend(came, bz)

    loads = [
        pltpu.make_async_copy(src, dst, R.w_sem.at[1 + i])
        for i, (src, dst) in enumerate(
            (
                (wg_ref, R.wg.at[:, pl.ds(0, HID // 2)]),
                (wu_ref, R.wu.at[:, pl.ds(0, HID // 2)]),
                (wd_ref, R.wd.at[pl.ds(0, HID // 2)]),
            )
        )
    ]
    taken = (
        (wg_ref, R.wg.at[:, pl.ds(HID // 2, HID // 2)]),
        (wu_ref, R.wu.at[:, pl.ds(HID // 2, HID // 2)]),
        (wd_ref, R.wd.at[pl.ds(HID // 2, HID // 2)]),
    )

    @pl.loop(0, NZ)
    def _(step):
        bz = behind(step)
        arrived("kh", step, spot(across, bz, 1 - k))
        attend(across, bz)

    for i, (src, dst) in enumerate(taken):
        loads[i].start()
        start(("twg", "twu", "twd")[i], 0, src, dst, {"k": 1 - k})

    slab = R.slab

    def strip(bx, bz, way=None):
        first = pl.multiple_of((bx * NZ + bz) * TOK, 16)
        if way is None:
            return slab.at[pl.ds(first, TOK)]
        return slab.at[pl.ds(pl.multiple_of(first + way * (TOK // 2), 16), TOK // 2)]

    for h in range(HEADS):
        at = pl.ds(h * TOK, TOK)
        att_ref[:, pl.ds(h * HEAD, HEAD)] = (R.acc[at, :HEAD] / R.acc[at, HEAD:]).astype(bf16)
    slab[pl.ds(pl.multiple_of((x * NZ + z) * TOK, 16), TOK), :] = att_ref[...]
    rows = strip(x, z)
    for step in range(1, NZ):
        start("az", step - 1, rows, rows, {"z": lax.rem(z + step, NZ)})
    for way, goes in enumerate(ways):
        start("ax", 0, rows, rows, {"x": goes})

    for b in range(NX * NZ):
        pair = [held[2 * b + core, POS:, :].astype(f32)[1:2, :FEATS] for core in range(2)]
        gains = jnp.concatenate(pair, axis=1)
        R.gain_squares[b] = 1.0 / (gains * gains)
    local_wo.wait()
    arrived("two", 0, R.wo.at[feats_of(1 - k)])
    arrived("tre", 0, R.res.at[feats_of(1 - k)])
    R.res_rows[...] = R.res[...].astype(f32).T.astype(bf16)

    for step in range(1, NZ):
        ref = strip(x, behind(step))
        arrived("az", step - 1, ref)
        for way, goes in enumerate(ways):
            start("ax", step, ref, ref, {"x": goes})

    def project_rows(bx):
        at = pl.ds(pl.multiple_of(bx * (NZ * TOK), 16), NZ * TOK)
        R.leaving[bx] = lax.dot_general(
            slab[at, :], R.wo[...], (((1,), (1,)), ((), ())), preferred_element_type=f32
        ).astype(bf16)
        for tw in range(2):
            here = (bx == y) & (tw == w)

            @pl.when(here)
            def _():
                R.pieces[own_expert] = R.leaving[bx, tw * 2 * TOK : (tw + 1) * 2 * TOK, :]

            @pl.when(jnp.logical_not(here))
            def _():
                piece = R.leaving.at[bx, pl.ds(tw * 2 * TOK, 2 * TOK)]
                start("ap", 0, piece, R.pieces.at[own_expert], {"y": bx, "w": tw})

    project_rows(x)
    for step in range(NZ):
        bz = behind(step)
        arrived("ax", step, slab.at[pl.ds(0, 2 * TOK)])
        for way, (came, goes) in enumerate(((down, up), (up, down))):
            ref = strip(came, bz, way)
            start("af", 0, ref, ref, {"x": goes})
    project_rows(up)
    project_rows(down)
    arrived("af", 0, slab.at[pl.ds(0, NZ * TOK)])
    project_rows(across)

    def token_rows(core, i):
        return pl.ds(pl.multiple_of(2 * TOK * i + core * TOK, 16), TOK)

    arrived("ap", 0, R.pieces.at[pl.ds(0, EXPERTS - 1)])
    total = jnp.concatenate([R.res_rows[token_rows(k, i), :] for i in range(2)], axis=0).astype(f32)
    for i in range(EXPERTS):
        total = total + R.pieces[i].astype(f32)
    R.stream[...] = total
    gain_pair = [
        held[2 * (x * NZ + z) + core, POS:, :].astype(f32)[1:2, :FEATS] for core in range(2)
    ]
    scaled = (total * jnp.concatenate(gain_pair, axis=1)).astype(bf16)

    for i in range(2):
        R.both[token_rows(k, i), :] = scaled[i * TOK : (i + 1) * TOK, :]
        ref = R.both.at[token_rows(k, i)]
        start("ab", 0, ref, ref, {"k": 1 - k})
    arrived("ab", 0, R.both.at[pl.ds(0, 2 * TOK)])

    def ahead(t):
        return lax.rem(t, 2) + 2 * (t // 4), lax.rem((t + 2) // 4, 2)

    def place(t):
        dy, dw = ahead(t)
        return lax.rem(y + dy, NY), lax.rem(w + dw, 2)

    def source(t):
        sy, sw = place(t)
        return 2 * sy + sw

    def place_rows(expert):
        at = pl.ds(pl.multiple_of(expert * SLOTS, 16), SLOTS)
        return jnp.dot(R.placer[at, :], R.both[...], preferred_element_type=f32).astype(bf16)

    def dispatch(t):
        dy, dw = ahead(t)
        dy = lax.rem(NY - dy, NY)
        ty, tw = lax.rem(y + dy, NY), lax.rem(w + dw, 2)
        e = 2 * ty + tw
        R.rows_out[e] = place_rows(e)
        start("dd", 2 * dy + dw, R.rows_out.at[e], R.rows_in.at[own_expert], {"y": ty, "w": tw})

    def cell(bx, bz):
        return bx * NZ + bz

    def half_of(ref, way):
        return ref.at[pl.ds(way * (SLOTS // 2), SLOTS // 2)]

    def keep_own(t):
        ys = source(t)
        return pltpu.make_async_copy(R.rows_in.at[ys], R.spread.at[ys, x * NZ + z], R.own_sem.at[t])

    def begin(t):
        ys = source(t)
        dy, dw = ahead(t)
        j = 2 * lax.rem(NY - dy, NY) + dw

        @pl.when(t > 0)
        def _():
            arrived("dd", j, R.rows_in.at[ys])

        keep_own(t).start()
        src, dst = R.rows_in.at[ys], R.spread.at[ys, x * NZ + z]
        for step in range(1, NZ):
            start("ez", t * 3 + step - 1, src, dst, {"z": lax.rem(z + step, NZ)})
        for way, goes in enumerate(ways):
            start("ex", t * 4, src, dst, {"x": goes})

    def along_x(t):
        ys = source(t)
        for step in range(1, NZ):
            ref = R.spread.at[ys, cell(x, behind(step))]
            arrived("ez", t * 3 + step - 1, ref)
            for way, goes in enumerate(ways):
                start("ex", t * 4 + step, ref, ref, {"x": goes})

    def pass_on(t):
        ys = source(t)
        for step in range(NZ):
            arrived("ex", t * 4 + step, R.from_x.at[ys, 0, pl.ds(0, 2)])
            for way, (came, goes) in enumerate(((down, up), (up, down))):
                ref = half_of(R.spread.at[ys, cell(came, behind(step))], way)
                start("ef", t, ref, ref, {"x": goes})

    def complete(t):
        ys = source(t)
        arrived("ef", t, R.spread.at[ys, pl.ds(across * NZ, NZ)])
        keep_own(t).wait()

    deep = 2 * WIDE

    def hidden(t):
        ys = source(t)
        R.gate_sum[...] = jnp.zeros_like(R.gate_sum)
        R.up_sum[...] = jnp.zeros_like(R.up_sum)
        R.squares[...] = jnp.zeros_like(R.squares)

        @pl.loop(0, D // deep)
        def _(i):
            at = pl.ds(pl.multiple_of(i * deep, 128), deep)
            piece = jnp.concatenate([R.spread[ys, 2 * i], R.spread[ys, 2 * i + 1]], axis=1)
            R.gate_sum[...] += jnp.dot(piece, R.wg[at, :], preferred_element_type=f32)
            R.up_sum[...] += jnp.dot(piece, R.wu[at, :], preferred_element_type=f32)
            wide = piece.astype(f32)
            wide = wide * wide
            wide = wide * jnp.concatenate([R.gain_squares[2 * i], R.gain_squares[2 * i + 1]], axis=1)
            total = wide[:, :128]
            for lane in range(128, deep, 128):
                total = total + wide[:, lane : lane + 128]
            R.squares[...] += total

        tile = 48

        @pl.loop(0, SLOTS // tile)
        def _(i):
            at = pl.ds(i * tile, tile)
            inverse = lax.rsqrt(jnp.sum(R.squares[at, :], axis=1, keepdims=True) / D + epsilon)
            gate = R.gate_sum[at, :] * inverse
            R.act[at, :] = (gate / (1.0 + jnp.exp(-gate)) * (R.up_sum[at, :] * inverse)).astype(bf16)

    def project(t, bx):
        ys = source(t)
        for i in range(NZ // 2):
            at = pl.ds(pl.multiple_of(bx * (NZ * WIDE) + i * deep, 128), deep)
            term = jnp.dot(R.act[...], R.wd[:, at], preferred_element_type=f32).astype(bf16)
            R.part[ys, cell(bx, 2 * i)] = term[:, :WIDE]
            R.part[ys, cell(bx, 2 * i + 1)] = term[:, WIDE:]

    def hand_out(t):
        ys = source(t)
        project(t, across)
        for step in range(NZ):
            for way, goes in enumerate(ways):
                ref = half_of(R.part.at[ys, cell(across, order[step])], way)
                start("er", t * 4 + step, ref, R.relay.at[ys, way, step], {"x": goes})
        for way, goes in enumerate(ways):
            project(t, goes)
            for step in range(NZ):
                ref = half_of(R.part.at[ys, cell(goes, order[step])], 1 - way)
                dst = half_of(R.from_x.at[ys, way, step], 1 - way)
                start("eu", t, ref, dst, {"x": goes})
        project(t, x)

    def add(dst, terms, count):
        tile = 48

        @pl.loop(0, count // tile)
        def _(i):
            at = pl.ds(i * tile, tile)
            total = terms[0][at, :].astype(f32)
            for term in terms[1:]:
                total = total + term[at, :].astype(f32)
            dst[at, :] = total.astype(dst.dtype)

    def add_relayed(t):
        ys = source(t)
        for step in range(NZ):
            arrived("er", t * 4 + step, R.rows_in.at[0])
            for way, goes in enumerate(ways):
                ref = R.relay.at[ys, way, step]
                add(ref, (ref, half_of(R.part.at[ys, cell(goes, order[step])], way)), SLOTS // 2)
                start("ev", t * 4 + step, ref, half_of(R.from_x.at[ys, way, step], way), {"x": goes})

    def x_terms(ys, step):
        own = R.part.at[ys, cell(x, order[step])]
        return [own, R.from_x.at[ys, 0, step], R.from_x.at[ys, 1, step]]

    def add_x(t):
        ys = source(t)
        arrived("eu", t, R.from_x.at[ys, 0])
        for step in range(NZ):
            arrived("ev", t * 4 + step, R.rows_in.at[0])
            if step < NZ - 1:
                mine = R.mine.at[ys, step]
                add(mine, x_terms(ys, step), SLOTS)
                start("eq", t, mine, R.from_z.at[ys, step], {"z": order[step]})

    def add_z(t):
        ys = source(t)
        arrived("eq", t, R.from_z.at[ys])
        terms = x_terms(ys, NZ - 1) + [R.from_z.at[ys, i] for i in range(NZ - 1)]

        @pl.when(t == 0)
        def _():
            add(R.returned.at[own_expert], terms, SLOTS)

        @pl.when(t > 0)
        def _():
            add(R.done.at[ys], terms, SLOTS)
            dy, dw = ahead(t)
            ty, tw = place(t)
            start("rt", 0, R.done.at[ys], R.returned.at[own_expert], {"y": ty, "w": tw})

    R.rows_in[own_expert] = place_rows(own_expert)
    begin(0)
    dispatch(1)
    dispatch(2)
    dispatch(3)
    begin(1)

    @pl.loop(0, STEPS + 5)
    def _(t):
        def stage(offset, what):
            @pl.when((t >= offset) & (t - offset < STEPS))
            def _():
                what(t - offset)

        stage(0, along_x)

        @pl.when(t + 4 < STEPS)
        def _():
            dispatch(t + 4)

        @pl.when(t + 2 < STEPS)
        def _():
            begin(t + 2)

        stage(1, pass_on)
        stage(4, add_x)
        stage(5, add_z)

        @pl.when(t == 2)
        def _():
            for i, (src, dst) in enumerate(taken):
                loads[i].wait()
                arrived(("twg", "twu", "twd")[i], 0, dst)

        def first(c):
            complete(c)
            hidden(c)

        stage(2, first)
        stage(3, add_relayed)
        stage(2, hand_out)

    arrived("rt", 0, R.returned.at[pl.ds(0, EXPERTS - 1)])
    results = R.returned[...].reshape(EXPERTS * SLOTS, WIDE)
    share = jnp.dot(R.picker[0], results, preferred_element_type=f32)
    share = share + jnp.dot(R.picker[1], results, preferred_element_type=f32)
    zero = jnp.zeros((TOK, WIDE), f32)
    parts = []
    for i in range(2):
        mine = R.stream[i * TOK : (i + 1) * TOK, :]
        parts += [jnp.where(k == 0, mine, zero), jnp.where(k == 0, zero, mine)]
    share = share + jnp.concatenate(parts, axis=0)
    first, second = share[:, :FEATS], share[:, FEATS:]
    R.give[...] = jnp.where(k == 0, second, first)
    start("ge", 0, R.give, R.got, {"k": 1 - k})
    keep = jnp.where(k == 0, first, second)
    arrived("ge", 0, R.got)
    mixed_ref[...] = (keep + R.got[...]).T.astype(bf16)

    for kind, many in (("kz", 3), ("kx", 8), ("kf", 4), ("kk", 12), ("kh", 4)):
        left(kind, held.at[pl.ds(0, many)])
    for kind, many in (("az", 3), ("ax", 8), ("af", 4)):
        left(kind, slab.at[pl.ds(0, many * TOK)])
    left("ap", R.pieces.at[pl.ds(0, EXPERTS - 1)])
    left("ab", R.both.at[pl.ds(0, 2 * TOK)])
    left("dd", R.rows_in.at[pl.ds(0, EXPERTS - 1)])
    left("rt", R.rows_in.at[pl.ds(0, EXPERTS - 1)])
    left("ge", R.give)
    left("two", R.wo.at[feats_of(0)])
    left("tre", R.res.at[feats_of(0)])
    for i, (src, dst) in enumerate(taken):
        left(("twg", "twu", "twd")[i], dst)
    left("ez", R.from_z)
    left("eq", R.from_z)
    left("ex", R.from_x)
    for kind in ("ef", "er", "eu", "ev"):
        left(kind, R.relay)


def local(
    queries,
    rotated_key_cache,
    value_cache_rows,
    kv_pos,
    q_pos,
    residual,
    w_out,
    norm_gain,
    routes,
    gate_probs,
    w_gate,
    w_up,
    w_down,
):
    any_spec, vmem_spec = pl.BlockSpec(memory_space=pl.ANY), pl.BlockSpec(memory_space=pltpu.VMEM)
    flops = 2 * STEPS * SLOTS * D * HID * 3
    attended, mixed = pl.pallas_call(
        layer_kernel,
        out_shape=(
            jax.ShapeDtypeStruct((TOK, JOINED), bf16),
            jax.ShapeDtypeStruct((FEATS, BLOCK), bf16),
        ),
        in_specs=[vmem_spec] * 7 + [any_spec] + [vmem_spec] * 2 + [any_spec] * 3,
        out_specs=(vmem_spec, vmem_spec),
        scratch_shapes=list(SCRATCH.values()),
        compiler_params=pltpu.CompilerParams(
            collective_id=1, has_side_effects=True, vmem_limit_bytes=63 << 20
        ),
        cost_estimate=pl.CostEstimate(flops=flops, bytes_accessed=20 << 20, transcendentals=0),
        name="layer",
    )(
        queries,
        q_pos[None, :],
        rotated_key_cache,
        value_cache_rows,
        kv_pos.reshape(2, 128),
        norm_gain[None, :],
        residual.T,
        w_out.T,
        routes.T,
        gate_probs.T,
        w_gate[0],
        w_up[0],
        w_down[0],
    )
    return attended, mixed.T


def solution(mesh):
    fine = Mesh(mesh.devices.reshape(NX, NZ, 2, 4, 2), ("x", "z", "k", "y", "w"))
    ctx, exp = ("x", "z", "k"), ("y", "w")
    in_specs = (
        P(ctx, exp),
        P(ctx, exp),
        P(ctx, exp),
        P(ctx),
        P(ctx),
        P(exp, ctx),
        P(exp, ctx),
        P(ctx),
        P(exp, None),
        P(exp, None),
        P(exp, None, ctx),
        P(exp, None, ctx),
        P(exp, ctx, None),
    )
    out_specs = (P(ctx, exp), P(exp, ctx))
    return jax.shard_map(local, mesh=fine, in_specs=in_specs, out_specs=out_specs, check_vma=False)
```

profile of v0, /device:TPU:1, one launch (start us, length us, event | category | flops | bytes accessed | tf_op | source)
XLA Modules:
  0.0 265.3 jit_solution(8935973809288272943)
XLA Ops:
  0.6 1.2 broadcast_in_dim.7.gain_ref
  1.9 260.4 %layer.1 = (bf16[64,768]{1,0:T(8,128)(2,1)}, bf16[192,256]{1,0:T(8,128)(2,1)}) custom-call(bf16[64,768]{1,0:T(8,128)(2,1)} %q_ref.1, s32[1,64]{1,0:T(1,128)} %bitcast.19, bf16[256,128]{1,0:T(8,128)(2,1)} %k_ref.1, bf16[256,128]{1,0:T(8,128)(2,1)} %v_ref.1, s32[2,128]{1,0:T(2,128)} %bitcast.18, bf16[1,192]{1,0:T(2,128)(2,1)} %broadcast_in_dim.7.gain_ref, ...), custom_call_target="tpu_custom_call" | custom-call | flops 14495514624 | bytes 20971520 | tf_op jit(solution)/shard_map/layer/pallas_call | solution.py:652
  262.2 1.5 copy.17
  263.8 1.5 copy.18
where the time goes:
time: 266 us; the launch traced here: 265 us
  Pallas kernels  260 us (98%)
  local copies, waits for them, and re-layouts  4.3 us (2%)
    pallas_call x1, Pallas kernels, local(): pl.pallas_call(layer_kernel, out_shape=(jax.ShapeDtypeStruct((TOK, JOINED...  260 us

commit v1 on v0

--- a/solution.py
+++ b/solution.py
@@ -68,8 +68,8 @@
     "own_sem": DMA((STEPS,)),
 }
 KINDS = {
-    "kz": 3, "kx": 4, "kf": 4, "kk": 8, "kh": 4,
-    "az": 3, "ax": 4, "af": 1, "ap": 1, "ab": 1,
+    "kz": 6, "kx": 8, "kf": 4, "kk": 8, "kh": 4,
+    "az": 6, "ax": 8, "af": 1, "ap": 1, "ab": 1,
     "dd": 8, "rt": 1, "ge": 1, "two": 1, "tre": 1, "twg": 1, "twu": 1, "twd": 1,
     "ez": 3 * STEPS, "ex": 4 * STEPS, "ef": STEPS,
     "er": 4 * STEPS, "eu": STEPS, "ev": 4 * STEPS, "eq": STEPS,
@@ -151,10 +151,12 @@
         return held.at[where, pl.ds(*halves[half])]
 
     block = spot(x, z, k)
-    for step in range(1, NZ):
-        start("kz", step - 1, block, block, {"z": lax.rem(z + step, NZ)})
-    for way, goes in enumerate(ways):
-        start("kx", 0, block, block, {"x": goes})
+    for part in range(2):
+        piece = spot(x, z, k, part)
+        for step in range(1, NZ):
+            start("kz", 2 * (step - 1) + part, piece, piece, {"z": lax.rem(z + step, NZ)})
+        for goes in ways:
+            start("kx", part, piece, piece, {"x": goes})
     start("kk", 0, block, block, {"k": 1 - k})
 
     def feats_of(core):
@@ -239,22 +241,25 @@
     arrived("kk", 0, spot(x, z, 1 - k))
     attend(x, z)
 
-    @pl.loop(1, NZ)
-    def _(step):
-        ref = spot(x, behind(step), k)
-        arrived("kz", step - 1, ref)
-        for way, goes in enumerate(ways):
-            start("kx", step, ref, ref, {"x": goes})
-        start("kk", step, ref, ref, {"k": 1 - k})
+    for part in range(2):
+        for step in range(1, NZ):
+            piece = spot(x, behind(step), k, part)
+            arrived("kz", 2 * (step - 1) + part, piece)
+            for goes in ways:
+                start("kx", 2 * step + part, piece, piece, {"x": goes})
+            if part == 1:
+                ref = spot(x, behind(step), k)
+                start("kk", step, ref, ref, {"k": 1 - k})
 
     @pl.loop(0, NZ)
     def _(step):
         bz = behind(step)
-        arrived("kx", step, held.at[pl.ds(0, 2)])
         for way, (came, goes) in enumerate(((down, up), (up, down))):
-            ref = spot(came, bz, k)
+            arrived("kx", 2 * step + way, held.at[pl.ds(0, 2), pl.ds(*halves[way])])
             half = spot(came, bz, k, way)
             start("kf", step, half, half, {"x": goes})
+        for came in (down, up):
+            ref = spot(came, bz, k)
             start("kk", NZ + step, ref, ref, {"k": 1 - k})
 
         @pl.when(step > 0)
@@ -311,10 +316,12 @@
         att_ref[:, pl.ds(h * HEAD, HEAD)] = (R.acc[at, :HEAD] / R.acc[at, HEAD:]).astype(bf16)
     slab[pl.ds(pl.multiple_of((x * NZ + z) * TOK, 16), TOK), :] = att_ref[...]
     rows = strip(x, z)
-    for step in range(1, NZ):
-        start("az", step - 1, rows, rows, {"z": lax.rem(z + step, NZ)})
-    for way, goes in enumerate(ways):
-        start("ax", 0, rows, rows, {"x": goes})
+    for part in range(2):
+        piece = strip(x, z, part)
+        for step in range(1, NZ):
+            start("az", 2 * (step - 1) + part, piece, piece, {"z": lax.rem(z + step, NZ)})
+        for goes in ways:
+            start("ax", part, piece, piece, {"x": goes})
 
     for b in range(NX * NZ):
         pair = [held[2 * b + core, POS:, :].astype(f32)[1:2, :FEATS] for core in range(2)]
@@ -325,11 +332,12 @@
     arrived("tre", 0, R.res.at[feats_of(1 - k)])
     R.res_rows[...] = R.res[...].astype(f32).T.astype(bf16)
 
-    for step in range(1, NZ):
-        ref = strip(x, behind(step))
-        arrived("az", step - 1, ref)
-        for way, goes in enumerate(ways):
-            start("ax", step, ref, ref, {"x": goes})
+    for part in range(2):
+        for step in range(1, NZ):
+            piece = strip(x, behind(step), part)
+            arrived("az", 2 * (step - 1) + part, piece)
+            for goes in ways:
+                start("ax", 2 * step + part, piece, piece, {"x": goes})
 
     def project_rows(bx):
         at = pl.ds(pl.multiple_of(bx * (NZ * TOK), 16), NZ * TOK)
@@ -351,8 +359,8 @@
     project_rows(x)
     for step in range(NZ):
         bz = behind(step)
-        arrived("ax", step, slab.at[pl.ds(0, 2 * TOK)])
         for way, (came, goes) in enumerate(((down, up), (up, down))):
+            arrived("ax", 2 * step + way, slab.at[pl.ds(0, TOK)])
             ref = strip(came, bz, way)
             start("af", 0, ref, ref, {"x": goes})
     project_rows(up)
@@ -559,6 +567,8 @@
     dispatch(2)
     dispatch(3)
     begin(1)
+    dispatch(4)
+    begin(2)
 
     @pl.loop(0, STEPS + 5)
     def _(t):
@@ -567,17 +577,17 @@
             def _():
                 what(t - offset)
 
+        stage(1, pass_on)
+
+        @pl.when(t + 5 < STEPS)
+        def _():
+            dispatch(t + 5)
+
+        @pl.when(t + 3 < STEPS)
+        def _():
+            begin(t + 3)
+
         stage(0, along_x)
-
-        @pl.when(t + 4 < STEPS)
-        def _():
-            dispatch(t + 4)
-
-        @pl.when(t + 2 < STEPS)
-        def _():
-            begin(t + 2)
-
-        stage(1, pass_on)
         stage(4, add_x)
         stage(5, add_z)
 

time: 266 us -> 258 us (0.970)
  Pallas kernels: 260 us -> 253 us
    pallas_call x1, Pallas kernels: 260 us -> 253 us  [local(): pl.pallas_call(layer_kernel, out_shape=(jax.ShapeDtypeStruct((TOK, JOINED...]
where the time goes in v1:
time: 258 us
  Pallas kernels  253 us (98%)
  local copies, waits for them, and re-layouts  4.3 us (2%)
    pallas_call x1, Pallas kernels, local(): pl.pallas_call(layer_kernel, out_shape=(jax.ShapeDtypeStruct((TOK, JOINED...  253 us

profile of v1, /device:TPU:1, one launch (start us, length us, event | category | flops | bytes accessed | tf_op | source)
XLA Modules:
  0.0 258.1 jit_solution(11968249653030936159)
XLA Ops:
  0.6 1.2 broadcast_in_dim.7.gain_ref
  1.9 253.2 %layer.1 = (bf16[64,768]{1,0:T(8,128)(2,1)}, bf16[192,256]{1,0:T(8,128)(2,1)}) custom-call(bf16[64,768]{1,0:T(8,128)(2,1)} %q_ref.1, s32[1,64]{1,0:T(1,128)} %bitcast.19, bf16[256,128]{1,0:T(8,128)(2,1)} %k_ref.1, bf16[256,128]{1,0:T(8,128)(2,1)} %v_ref.1, s32[2,128]{1,0:T(2,128)} %bitcast.18, bf16[1,192]{1,0:T(2,128)(2,1)} %broadcast_in_dim.7.gain_ref, ...), custom_call_target="tpu_custom_call" | custom-call | flops 14495514624 | bytes 20971520 | tf_op jit(solution)/shard_map/layer/pallas_call | solution.py:662
  255.0 1.5 copy.17
  256.6 1.5 copy.18
